TPU v7x, 256 devices: a whole 4x4x8 slice. The times are simulated.
256 devices in a mesh: gx: 8 (over x, core), gy: 8 (over z), gz: 4 (over y).
Axes of the slice: x: 4, y: 4, z: 8, core: 2. Of those that a mesh axis runs over, the one named last changes fastest.
Arguments:
- spectrum: bfloat16 [256, 256, 32, 256], P('gx', 'gy', 'gz'), may hold values from 0.049804688 to 2
- wind_east: float32 [256, 256, 32], P('gx', 'gy', 'gz'), may hold values from -0.45 to 0.45
- wind_north: float32 [256, 256, 32], P('gx', 'gy', 'gz'), may hold values from -0.45 to 0.45
- fall_rate: float32 [32, 256], P('gz'), may hold values from 0.006 to 12
- cloud_cells: int32 [8, 8, 4, 64, 16], P('gx', 'gy', 'gz'), may hold values from 0 to 8191, as said below
- block_target: int32 [8, 8, 4, 64], P(None, None, 'gz'), may hold values from 0 to 64, as said below
- pair_inputs: bfloat16 [256, 2048], replicated, may hold values from -0.375 to 0.375
- pair_outputs: bfloat16 [1024, 256], replicated, may hold values from -0.1875 to 0.1875
- loss_kernel: bfloat16 [256, 256], replicated, may hold values from 0 to 0.00390625
- fragments: bfloat16 [256, 256], replicated, may hold values from 0 to 0.0078125
Outputs:
- settled: bfloat16 [256, 256, 32, 256], P('gx', 'gy', 'gz')
Inputs may be any that keep to these rules, and one draw needn't show every extreme that they name: `cloud_cells`: entry [i, j, k, b, :] lists the local cell numbers (x * 32 + y) * 8 + z of block b of the device at mesh index (i, j, k); the 1024 entries of one device are distinct. `block_target`: entry [i, j, k, b] below 64 is the flat index i2 * (devices along gy) + j2 of the device (i2, j2, k) that works on block b of device (i, j, k); 64 marks a block without cloud. In each gz index the cloudy blocks number 64 * 32 in all, a device holds 1 to 64 of them, every device of the plane is named exactly 32 times, and by at most 1 block of any one device.
All inputs are finite; a program needn't handle non-finite values.
Results may differ from a plain program's by a relative error of at most 0.0032.
Values may be sent and summed in bfloat16 or wider, within the bound.
No kernel may reach another device: no remote copies, remote signals or barrier semaphores. Data moves between devices by JAX's collectives and lax.ppermute only.
A program may use at most 128 MiB of HBM per device.

v0:
```python
import jax
import jax.numpy as jnp
from jax import lax
from jax.sharding import PartitionSpec as P


def padded_2(x, sides, width):
    edges = {}
    for axis, dim in sides:
        size, length = (lax.axis_size(axis), x.shape[dim])
        up = [(i, (i + 1) % size) for i in range(size)]
        last = lax.slice_in_dim(x, length - width, length, axis=dim)
        initial = lax.slice_in_dim(x, 0, width, axis=dim)
        edges[dim] = (
            lax.ppermute(last, axis, up),
            lax.ppermute(initial, axis, [(b, a) for a, b in up]),
        )
    done = []
    for _, dim in sides:
        low, high = edges[dim]
        around = [(width, width) if d in done else (0, 0) for d in range(x.ndim)]
        x = jnp.concatenate([jnp.pad(low, around), x, jnp.pad(high, around)], axis=dim)
        done.append(dim)
    return x


def collide(cloud_rows, pair_inputs, pair_outputs, loss_kernel, fragments):
    pair_count = pair_outputs.shape[0]
    linear = jnp.dot(cloud_rows, pair_inputs, preferred_element_type=jnp.float32)
    products = (linear[:, :pair_count] * linear[:, pair_count:]).astype(jnp.bfloat16)
    decline = jnp.dot(cloud_rows, loss_kernel, preferred_element_type=jnp.float32)
    losses = cloud_rows.astype(jnp.float32) * decline
    gained = jnp.dot(products, pair_outputs, preferred_element_type=jnp.float32)
    gained = gained + jnp.dot(
        losses.astype(jnp.bfloat16), fragments, preferred_element_type=jnp.float32
    )
    return (gained - losses).astype(jnp.bfloat16)


def advect(spectrum, wind_east, wind_north):
    padded = padded_2(spectrum, (("gx", 0), ("gy", 1)), 1)
    centre = spectrum.astype(jnp.float32)
    from_west = padded[:-2, 1:-1].astype(jnp.float32)
    from_east = padded[2:, 1:-1].astype(jnp.float32)
    from_south = padded[1:-1, :-2].astype(jnp.float32)
    from_north = padded[1:-1, 2:].astype(jnp.float32)
    east_rate = wind_east[..., None]
    north_rate = wind_north[..., None]
    return (
        centre
        - jnp.maximum(east_rate, 0.0) * (centre - from_west)
        - jnp.minimum(east_rate, 0.0) * (from_east - centre)
        - jnp.maximum(north_rate, 0.0) * (centre - from_south)
        - jnp.minimum(north_rate, 0.0) * (from_north - centre)
    )


def segment_maps(fall_rate):
    levels, channels = fall_rate.shape
    inverse = 1.0 / (1.0 + fall_rate)
    rows = [None] * levels
    gains = [None] * levels
    above_row = jnp.zeros((levels, channels), jnp.float32)
    above_gain = jnp.ones((channels,), jnp.float32)
    level_ids = jnp.arange(levels)[:, None]
    for level_index in reversed(range(levels)):
        own_row = jnp.where(level_ids == level_index, 1.0, 0.0).astype(jnp.float32)
        row = inverse[level_index][None, :] * (own_row + above_row)
        gain = inverse[level_index] * above_gain
        rows[level_index] = row
        gains[level_index] = gain
        above_row = fall_rate[level_index][None, :] * row
        above_gain = fall_rate[level_index] * gain
    return (jnp.stack(rows, axis=0), jnp.stack(gains, axis=0), above_row, above_gain)


def body(
    spectrum,
    wind_east,
    wind_north,
    fall_rate,
    cloud_cells,
    block_target,
    pair_inputs,
    pair_outputs,
    loss_kernel,
    fragments,
):
    size_x, size_y, size_z, channels = spectrum.shape
    number_of_cells = size_x * size_y * size_z
    advected = advect(spectrum, wind_east, wind_north)
    flat_cells = advected.reshape(number_of_cells, channels)
    blocks_total = cloud_cells.shape[3]
    block_cells = cloud_cells.shape[4]
    cell_ids = cloud_cells.reshape(blocks_total * block_cells)
    blocks = flat_cells[cell_ids].astype(jnp.bfloat16).reshape(blocks_total, block_cells, channels)
    plane_size = lax.axis_size("gx") * lax.axis_size("gy")
    own_index = lax.axis_index("gx") * lax.axis_size("gy") + lax.axis_index("gy")
    routes = block_target.reshape(plane_size, blocks_total)
    own_targets = lax.dynamic_index_in_dim(routes, own_index, 0, keepdims=False)
    active = own_targets < plane_size
    zero_value = jnp.zeros((), jnp.bfloat16)
    computed = collide(
        blocks.reshape(-1, channels), pair_inputs, pair_outputs, loss_kernel, fragments
    )
    tendency = jnp.where(
        active[:, None, None], computed.reshape(blocks_total, block_cells, channels), zero_value
    )
    moist_field = (
        flat_cells.at[cell_ids]
        .add(tendency.reshape(-1, channels).astype(jnp.float32))
        .reshape(size_x, size_y, size_z, channels)
    )
    level_rows, level_gains, out_row, carried_gain = segment_maps(fall_rate)
    local_values = jnp.zeros((size_x, size_y, size_z, channels), jnp.float32)
    inflow = jnp.zeros((size_x, size_y, channels), jnp.float32)
    for source in range(size_z):
        source_level = moist_field[:, :, source : source + 1, :]
        local_values = local_values + source_level * level_rows[:, source, :]
        inflow = inflow + source_level[:, :, 0, :] * out_row[source]
    all_flux, all_gain = (
        lax.all_gather(inflow[None].astype(jnp.bfloat16), "gz", axis=0, tiled=True).astype(
            jnp.float32
        ),
        lax.all_gather(carried_gain[None].astype(jnp.bfloat16), "gz", axis=0, tiled=True).astype(
            jnp.float32
        ),
    )
    height = lax.axis_size("gz")
    own_level = lax.axis_index("gz")
    incoming = jnp.zeros_like(inflow)
    for upper in reversed(range(height)):
        incoming = jnp.where(
            upper > own_level, all_flux[upper] + all_gain[upper] * incoming, incoming
        )
    return (local_values + incoming[:, :, None, :] * level_gains).astype(jnp.bfloat16)


def solution(mesh):
    in_specs = (
        P("gx", "gy", "gz", None),
        P("gx", "gy", "gz"),
        P("gx", "gy", "gz"),
        P("gz", None),
        P("gx", "gy", "gz", None, None),
        P(None, None, "gz", None),
        P(),
        P(),
        P(),
        P(),
    )
    out_specs = P("gx", "gy", "gz", None)
    return jax.shard_map(body, mesh=mesh, in_specs=in_specs, out_specs=out_specs, check_vma=False)
```

profile of v0, /device:TPU:1, one launch (start us, length us, event | category | flops | bytes accessed | tf_op | source)
XLA Modules:
  0.0 160.9 jit_solution(9245047635911674080)
XLA Ops:
  6.5 1.8 %fusion.58 = (bf16[1,32,8,256]{3,2,1,0:T(8,128)(2,1)}, bf16[1,32,8,256]{3,2,1,0:T(8,128)(2,1)}) fusion(bf16[32,32,8,256]{3,2,1,0:T(8,128)(2,1)} %param.10), kind=kLoop, calls=%fused_computation.129 | loop fusion | bytes 524288 | tf_op jit(solution)/shard_map/slice | solution.py:13
  8.3 2.6 %collective-permute-start = (bf16[1,32,8,256]{3,2,1,0:T(8,128)(2,1)}, bf16[1,32,8,256]{3,2,1,0:T(8,128)(2,1)S(1)}, u32[]{:S(2)}, u32[]{:S(2)}) collective-permute-start(bf16[1,32,8,256]{3,2,1,0:T(8,128)(2,1)} %get-tuple-element.24), channel_id=1, source_target_pairs={{0,32},{32,64},{64,96},{96,128},{128,160},{160,192},{192,224},{224... | collective-permute-start | bytes 393224 | tf_op jit(solution)/shard_map/ppermute | solution.py:15
  11.5 1.7 %fusion.57 = (bf16[32,1,8,256]{3,2,1,0:T(8,128)(2,1)}, bf16[32,1,8,256]{3,2,1,0:T(8,128)(2,1)}) fusion(bf16[32,32,8,256]{3,2,1,0:T(8,128)(2,1)} %param.10), kind=kLoop, calls=%fused_computation.128 | loop fusion | bytes 524288 | tf_op jit(solution)/shard_map/slice | solution.py:12
  13.2 1.0 collective-permute-start.2
  14.2 3.9 %collective-permute-start.3 = (bf16[32,1,8,256]{3,2,1,0:T(8,128)(2,1)}, bf16[32,1,8,256]{3,2,1,0:T(8,128)(2,1)}, u32[]{:S(2)}, u32[]{:S(2)}) collective-permute-start(bf16[32,1,8,256]{3,2,1,0:T(8,128)(2,1)} %get-tuple-element.22), channel_id=1, source_target_pairs={{4,0},{8,4},{12,8},{16,12},{20,16},{24,20},{28,24},{0,28},{5,1},{9... | collective-permute-start | bytes 393224 | tf_op jit(solution)/shard_map/ppermute | solution.py:16
  18.2 0.7 add_divide_fusion
  19.5 1.6 %convert_bitcast_fusion = (bf16[1,1,256]{2,1,0:T(2,128)(2,1)}, f32[1,256]{1,0:T(1,128)}, f32[1,256]{1,0:T(1,128)}, f32[1,256]{1,0:T(1,128)}, f32[1,256]{1,0:T(1,...) fusion(f32[8,256]{1,0:T(8,128)} %param.13, ...), kind=kLoop, calls=%fused_computation.119 | loop fusion | flops 4096 | bytes 27136
  21.1 1.6 fusion.61
  24.9 0.9 broadcast_maximum_fusion.1
  26.3 0.9 broadcast_maximum_fusion
  27.7 0.8 copy.43
  28.6 0.7 compare_bitcast_fusion
  30.0 1.6 constant_dynamic-update-slice_fusion.10
  31.6 0.8 multiply_multiply_fusion.1
  33.0 1.4 constant_dynamic-update-slice_fusion.9
  35.1 2.5 %constant_dynamic-update-slice_fusion.1 = bf16[34,32,8,256]{3,2,1,0:T(8,128)(2,1)S(1)} fusion(bf16[34,32,8,256]{3,2,1,0:T(8,128)(2,1)S(1)} %constant_dynamic-update-slice_fusion.2, bf16[32,32,8,256]{3,2,1,0:T(8,128)(2,1)} %param.10), kind=kLoop, calls=%fused_computation.76 | loop fusion | bytes 8388608
  37.6 12.5 %fusion.3 = f32[32,32,8,256]{3,2,1,0:T(8,128)} fusion(bf16[32,32,8,256]{3,2,1,0:T(8,128)(2,1)S(1)} %copy-done.1, bf16[34,32,8,256]{3,2,1,0:T(8,128)(2,1)S(1)} %constant_dynamic-update-slice_fusion, bf16[32,1,8,256]{3,2,1,0:T(8,128)(2,1)} %collective-permute-done.3, bf16[32,1,8,256]{3,2,1,0:T(8,128)(2,1)} %collective-permute-done.2, ...), kind=kLoop, calls=%fused_computation.10 | loop fusion | flops 73400320 | bytes 17694720 | tf_op jit(solution)/shard_map/sub | solution.py:50
  50.1 7.4 %gather_fusion = bf16[1024,256]{1,0:T(8,128)(2,1)S(1)} fusion(f32[8192,256]{1,0:T(8,128)} %bitcast.160, s32[1024]{0:T(1024)} %broadcast_clamp_fusion), kind=kCustom, calls=%fused_computation | custom fusion | bytes 1052672 | tf_op jit(solution)/shard_map/gather | solution.py:96
  57.8 1.3 fusion.64
  59.4 1.0 fusion.26
  60.5 12.7 %scatter_fusion = f32[8192,256]{1,0:T(8,128)} fusion(f32[8192,256]{1,0:T(8,128)} %bitcast.161, s32[1024]{0:T(1024)S(1)} %bitcast.215, f32[1024,256]{1,0:T(8,128)S(1)} %fusion.26), kind=kCustom, calls=%fused_computation.1 | custom fusion | flops 262144 | bytes 3149824 | tf_op jit(solution)/shard_map/scatter-add | solution.py:111
  73.3 30.4 %fusion.56 = (f32[32,32,1,256]{3,2,1,0:T(1,128)S(1)}, f32[32,32,1,256]{3,2,1,0:T(1,128)S(1)}, f32[32,32,1,256]{3,2,1,0:T(1,128)S(1)}, f32[32,32,1,256]{3,2,1,0:T...) fusion(f32[32,32,8,256]{3,2,1,0:T(8,128)} %bitcast.162), kind=kLoop, calls=%fused_computation.127 | loop fusion | bytes 16777216 | tf_op jit(solution)/shard_map/slice | solution.py:118
  103.9 0.7 copy-done.2
  106.4 1.9 %fusion.38 = bf16[1,32,32,256]{3,2,1,0:T(8,128)(2,1)} fusion(f32[32,32,1,256]{3,2,1,0:T(1,128)S(1)} %get-tuple-element.20, f32[32,32,1,256]{3,2,1,0:T(1,128)S(1)} %get-tuple-element.14, f32[32,32,1,256]{3,2,1,0:T(1,128)S(1)} %get-tuple-element.15, f32[32,32,1,256]{3,2,1,0:T(1,128)S(1)} %get-tuple-element.16, f32[32,32,1,256]{3,2,1,0:T(1,128)S(1)} %get-tuple-element.17, ...), kind=kLoop, calls=%fused_computation.45 | loop fusion | flops 4194304 | bytes 8921088 | tf_op jit(solution)/shard_map/convert_element_type | solution.py:122
  108.6 8.0 %all-gather = bf16[4,1,256]{2,1,0:T(2,128)(2,1)S(1)} all-gather(bf16[1,1,256]{2,1,0:T(2,128)(2,1)S(1)} %copy-done.53), channel_id=1, replica_groups=mesh['gx'=8,'gy'=8,'gz'=4] {'gz'}, dimensions={0}, use_global_device_ids=true | all-gather | bytes 2560 | tf_op jit(solution)/shard_map/all_gather | solution.py:125
  117.2 3.3 %copy_bitcast_fusion.6 = (f32[32,32,256]{2,1,0:T(8,128)}, f32[32,32,256]{2,1,0:T(8,128)}) fusion(f32[32,32,1,256]{3,2,1,0:T(1,128)} %copy-done.9, f32[32,32,1,256]{3,2,1,0:T(1,128)} %copy-done.8), kind=kLoop, calls=%fused_computation.66 | loop fusion | bytes 4194304 | tf_op jit(solution)/shard_map/mul | solution.py:119
  120.5 3.3 %copy_bitcast_fusion.4 = (f32[32,32,256]{2,1,0:T(8,128)}, f32[32,32,256]{2,1,0:T(8,128)}) fusion(f32[32,32,1,256]{3,2,1,0:T(1,128)} %copy-done.6, f32[32,32,1,256]{3,2,1,0:T(1,128)} %copy-done.7), kind=kLoop, calls=%fused_computation.64 | loop fusion | bytes 4194304 | tf_op jit(solution)/shard_map/mul | solution.py:119
  123.8 1.5 copy_bitcast_fusion.2
  125.3 1.5 copy_bitcast_fusion
  126.8 15.7 %all-gather.3.cloned.1.call-done = bf16[4,32,32,256]{3,2,1,0:T(8,128)(2,1)} async-done(((bf16[1,32,32,256]{3,2,1,0:T(8,128)(2,1)}), bf16[4,32,32,256]{3,2,1,0:T(8,128)(2,1)}) %all-gather.3.cloned.1.call-update) | async-done | bytes 2097168 | tf_op jit(solution)/shard_map/all_gather | solution.py:122
  142.5 2.2 %convert_element_type.73 = f32[4,32,32,256]{3,2,1,0:T(8,128)S(1)} convert(bf16[4,32,32,256]{3,2,1,0:T(8,128)(2,1)} %all-gather.3.cloned.1.call-done) | non-fusion elementwise | flops 1048576 | bytes 6291456 | tf_op jit(solution)/shard_map/convert_element_type | solution.py:122
  146.0 8.1 %add_convert_fusion = bf16[32,32,8,256]{3,2,1,0:T(8,128)(2,1)} fusion(f32[8,256]{1,0:T(8,128)S(1)} %stack.5, f32[32,32,256]{2,1,0:T(8,128)S(1)} %fusion.36, f32[8,256]{1,0:T(8,128)S(1)} %bitcast.226, f32[32,32,256]{2,1,0:T(8,128)S(1)} %copy-done.16, f32[8,256]{1,0:T(8,128)S(1)} %bitcast.227, f32[32,32,256]{2,1,0:T(8,128)S(1)} %copy-done.17, ...), kind=kLoop, calls=%fused_computation.16 | loop fusion | flops 37748736 | bytes 13705216 | tf_op jit(solution)/shard_map/convert_element_type | solution.py:136
  (153 shorter events, 10.6 us)
Async XLA Ops:
  6.5 51.3 %copy-start = (bf16[256,2048]{1,0:T(8,128)(2,1)S(1)}, bf16[256,2048]{1,0:T(8,128)(2,1)}, u32[]{:S(2)}) copy-start(bf16[256,2048]{1,0:T(8,128)(2,1)} %param.16) | copy-start | bytes 3145732
  6.5 136.0 %all-gather.3.cloned.1.call-start = ((), (), s32[]{:S(2)}) async-start(), calls=%async_computation | async-start | bytes 2621440 | tf_op jit(solution)/shard_map/all_gather | solution.py:122
  8.3 26.8 %collective-permute-start = (bf16[1,32,8,256]{3,2,1,0:T(8,128)(2,1)}, bf16[1,32,8,256]{3,2,1,0:T(8,128)(2,1)S(1)}, u32[]{:S(2)}, u32[]{:S(2)}) collective-permute-start(bf16[1,32,8,256]{3,2,1,0:T(8,128)(2,1)} %get-tuple-element.24), channel_id=1, source_target_pairs={{0,32},{32,64},{64,96},{96,128},{128,160},{160,192},{192,224},{224... | collective-permute-start | bytes 393224 | tf_op jit(solution)/shard_map/ppermute | solution.py:15
  10.9 26.6 %collective-permute-start.1 = (bf16[1,32,8,256]{3,2,1,0:T(8,128)(2,1)}, bf16[1,32,8,256]{3,2,1,0:T(8,128)(2,1)S(1)}, u32[]{:S(2)}, u32[]{:S(2)}) collective-permute-start(bf16[1,32,8,256]{3,2,1,0:T(8,128)(2,1)} %get-tuple-element.23), channel_id=1, source_target_pairs={{32,0},{64,32},{96,64},{128,96},{160,128},{192,160},{224,192},{0,2... | collective-permute-start | bytes 393224 | tf_op jit(solution)/shard_map/ppermute | solution.py:16
  13.2 24.4 %collective-permute-start.2 = (bf16[32,1,8,256]{3,2,1,0:T(8,128)(2,1)}, bf16[32,1,8,256]{3,2,1,0:T(8,128)(2,1)}, u32[]{:S(2)}, u32[]{:S(2)}) collective-permute-start(bf16[32,1,8,256]{3,2,1,0:T(8,128)(2,1)} %get-tuple-element.21), channel_id=1, source_target_pairs={{0,4},{4,8},{8,12},{12,16},{16,20},{20,24},{24,28},{28,0},{1,5},{5... | collective-permute-start | bytes 393224 | tf_op jit(solution)/shard_map/ppermute | solution.py:15
  14.2 23.4 %collective-permute-start.3 = (bf16[32,1,8,256]{3,2,1,0:T(8,128)(2,1)}, bf16[32,1,8,256]{3,2,1,0:T(8,128)(2,1)}, u32[]{:S(2)}, u32[]{:S(2)}) collective-permute-start(bf16[32,1,8,256]{3,2,1,0:T(8,128)(2,1)} %get-tuple-element.22), channel_id=1, source_target_pairs={{4,0},{8,4},{12,8},{16,12},{20,16},{24,20},{28,24},{0,28},{5,1},{9... | collective-permute-start | bytes 393224 | tf_op jit(solution)/shard_map/ppermute | solution.py:16
  28.6 9.0 %copy-start.26 = (s32[1024,1]{0,1:T(1,128)}, s32[1024,1]{0,1:T(1,128)S(1)}, u32[]{:S(2)}) copy-start(s32[1024,1]{0,1:T(1,128)S(1)} %compare_select_fusion) | copy-start | bytes 12292
  30.0 7.6 %copy-start.1 = (bf16[32,32,8,256]{3,2,1,0:T(8,128)(2,1)S(1)}, bf16[32,32,8,256]{3,2,1,0:T(8,128)(2,1)}, u32[]{:S(2)}) copy-start(bf16[32,32,8,256]{3,2,1,0:T(8,128)(2,1)} %param.10) | copy-start | bytes 12582916
  37.6 19.9 %copy-start.19 = (bf16[256,256]{1,0:T(8,128)(2,1)S(1)}, bf16[256,256]{1,0:T(8,128)(2,1)}, u32[]{:S(2)}) copy-start(bf16[256,256]{1,0:T(8,128)(2,1)} %param.18) | copy-start | bytes 393220
  50.1 9.0 %copy-start.20 = (bf16[256,256]{1,0:T(8,128)(2,1)S(1)}, bf16[256,256]{1,0:T(8,128)(2,1)}, u32[]{:S(2)}) copy-start(bf16[256,256]{1,0:T(8,128)(2,1)} %param.19) | copy-start | bytes 393220
  73.2 33.1 %copy-start.37 = (f32[1,256]{1,0:T(1,128)S(1)}, f32[1,256]{1,0:T(1,128)}, u32[]{:S(2)}) copy-start(f32[1,256]{1,0:T(1,128)} %get-tuple-element.37) | copy-start | bytes 3076
  73.2 33.1 %copy-start.38 = (f32[1,256]{1,0:T(1,128)S(1)}, f32[1,256]{1,0:T(1,128)}, u32[]{:S(2)}) copy-start(f32[1,256]{1,0:T(1,128)} %get-tuple-element.38) | copy-start | bytes 3076
  73.2 33.1 %copy-start.39 = (f32[1,256]{1,0:T(1,128)S(1)}, f32[1,256]{1,0:T(1,128)}, u32[]{:S(2)}) copy-start(f32[1,256]{1,0:T(1,128)} %get-tuple-element.39) | copy-start | bytes 3076
  73.2 33.1 %copy-start.40 = (f32[1,256]{1,0:T(1,128)S(1)}, f32[1,256]{1,0:T(1,128)}, u32[]{:S(2)}) copy-start(f32[1,256]{1,0:T(1,128)} %get-tuple-element.40) | copy-start | bytes 3076
  73.2 33.1 %copy-start.41 = (f32[1,256]{1,0:T(1,128)S(1)}, f32[1,256]{1,0:T(1,128)}, u32[]{:S(2)}) copy-start(f32[1,256]{1,0:T(1,128)} %get-tuple-element.41) | copy-start | bytes 3076
  73.2 33.1 %copy-start.42 = (f32[1,256]{1,0:T(1,128)S(1)}, f32[1,256]{1,0:T(1,128)}, u32[]{:S(2)}) copy-start(f32[1,256]{1,0:T(1,128)} %get-tuple-element.42) | copy-start | bytes 3076
  73.3 33.1 %copy-start.43 = (f32[1,256]{1,0:T(1,128)S(1)}, f32[1,256]{1,0:T(1,128)}, u32[]{:S(2)}) copy-start(f32[1,256]{1,0:T(1,128)} %get-tuple-element.43) | copy-start | bytes 3076
  73.3 33.1 %copy-start.44 = (f32[1,256]{1,0:T(1,128)S(1)}, f32[1,256]{1,0:T(1,128)}, u32[]{:S(2)}) copy-start(f32[1,256]{1,0:T(1,128)} %get-tuple-element.44) | copy-start | bytes 3076
  103.7 4.6 %copy-start.21 = (f32[8,8,256]{2,1,0:T(8,128)S(1)}, f32[8,8,256]{2,1,0:T(8,128)}, u32[]{:S(2)}) copy-start(f32[8,8,256]{2,1,0:T(8,128)} %constant_dynamic-update-slice_fusion.9) | copy-start | bytes 196612
  103.7 4.6 %copy-start.22 = (f32[1,256]{1,0:T(1,128)S(1)}, f32[1,256]{1,0:T(1,128)}, u32[]{:S(2)}) copy-start(f32[1,256]{1,0:T(1,128)} %get-tuple-element.58) | copy-start | bytes 3076
  103.9 4.7 %copy-start.53 = (bf16[1,1,256]{2,1,0:T(2,128)(2,1)S(1)}, bf16[1,1,256]{2,1,0:T(2,128)(2,1)}, u32[]{:S(2)}) copy-start(bf16[1,1,256]{2,1,0:T(2,128)(2,1)} %get-tuple-element.5) | copy-start | bytes 1540
  103.9 13.2 %copy-start.46 = (f32[1,256]{1,0:T(1,128)S(1)}, f32[1,256]{1,0:T(1,128)}, u32[]{:S(2)}) copy-start(f32[1,256]{1,0:T(1,128)} %get-tuple-element.6) | copy-start | bytes 3076
  103.9 13.2 %copy-start.47 = (f32[1,256]{1,0:T(1,128)S(1)}, f32[1,256]{1,0:T(1,128)}, u32[]{:S(2)}) copy-start(f32[1,256]{1,0:T(1,128)} %get-tuple-element.7) | copy-start | bytes 3076
  103.9 13.2 %copy-start.48 = (f32[1,256]{1,0:T(1,128)S(1)}, f32[1,256]{1,0:T(1,128)}, u32[]{:S(2)}) copy-start(f32[1,256]{1,0:T(1,128)} %get-tuple-element.8) | copy-start | bytes 3076
  103.9 13.2 %copy-start.49 = (f32[1,256]{1,0:T(1,128)S(1)}, f32[1,256]{1,0:T(1,128)}, u32[]{:S(2)}) copy-start(f32[1,256]{1,0:T(1,128)} %get-tuple-element.9) | copy-start | bytes 3076
  103.9 13.2 %copy-start.50 = (f32[1,256]{1,0:T(1,128)S(1)}, f32[1,256]{1,0:T(1,128)}, u32[]{:S(2)}) copy-start(f32[1,256]{1,0:T(1,128)} %get-tuple-element.10) | copy-start | bytes 3076
  103.9 13.2 %copy-start.51 = (f32[1,256]{1,0:T(1,128)S(1)}, f32[1,256]{1,0:T(1,128)}, u32[]{:S(2)}) copy-start(f32[1,256]{1,0:T(1,128)} %get-tuple-element.11) | copy-start | bytes 3076
  103.9 13.2 %copy-start.52 = (f32[1,256]{1,0:T(1,128)S(1)}, f32[1,256]{1,0:T(1,128)}, u32[]{:S(2)}) copy-start(f32[1,256]{1,0:T(1,128)} %get-tuple-element.12) | copy-start | bytes 3076
  117.2 6.6 %copy-start.3 = (f32[32,32,1,256]{3,2,1,0:T(1,128)S(1)}, f32[32,32,1,256]{3,2,1,0:T(1,128)}, u32[]{:S(2)}) copy-start(f32[32,32,1,256]{3,2,1,0:T(1,128)} %copy-done.2) | copy-start | bytes 3145732
  117.2 6.6 %copy-start.5 = (f32[32,32,1,256]{3,2,1,0:T(1,128)S(1)}, f32[32,32,1,256]{3,2,1,0:T(1,128)}, u32[]{:S(2)}) copy-start(f32[32,32,1,256]{3,2,1,0:T(1,128)} %copy-done.4) | copy-start | bytes 3145732
  126.8 18.6 %copy-start.10 = (f32[32,32,256]{2,1,0:T(8,128)S(1)}, f32[32,32,256]{2,1,0:T(8,128)}, u32[]{:S(2)}) copy-start(f32[32,32,256]{2,1,0:T(8,128)} %get-tuple-element.78) | copy-start | bytes 3145732
  126.8 18.6 %copy-start.11 = (f32[32,32,256]{2,1,0:T(8,128)S(1)}, f32[32,32,256]{2,1,0:T(8,128)}, u32[]{:S(2)}) copy-start(f32[32,32,256]{2,1,0:T(8,128)} %get-tuple-element.79) | copy-start | bytes 3145732
  (27 other events, 89.9 us)
Sparse Core Ops, SparseCore 0:
  108.5 34.0 all-gather.2
where the time goes:
time: 162 us; the launch traced here: 161 us
  local copies, waits for them, and re-layouts  61.7 us (38%)
  other arithmetic  50.1 us (31%)
  waiting for transfers between devices  15.7 us (10%)
  between operations  14.3 us (9%)
  starting transfers between devices  8.19 us (5%)
  blocking collectives  7.95 us (5%)
  matrix products  2.91 us (2%)
    slice x1, local copies, waits for them, and re-layouts, body(): source_level = moist_field[:, :, source:source + 1, :]  30.4 us
    all_gather x1, waiting for transfers between devices, body(): lax.all_gather(inflow[None].astype(jnp.bfloat16), 'gz', axis=0, tiled=True)  15.7 us
    scatter-add x1, other arithmetic, body(): moist_field = flat_cells.at[cell_ids].add(tendency.reshape(-1, channels)....  12.7 us
    sub x1, other arithmetic, advect(): centre - jnp.maximum(east_rate, 0.0) * (centre - from_west)  12.5 us
    mul x4, local copies, waits for them, and re-layouts, body(): local_values = local_values + source_level * level_rows[:, source, :]  9.6 us
    convert_element_type x1, other arithmetic, body(): (local_values + incoming[:, :, None, :] * level_gains).astype(jnp.bfloat16)  8.12 us
    all_gather x1, blocking collectives, body(): lax.all_gather(carried_gain[None].astype(jnp.bfloat16), 'gz', axis=0, til...  7.95 us
    gather x1, local copies, waits for them, and re-layouts, body(): flat_cells[cell_ids].astype(jnp.bfloat16)  7.36 us
  transfers between devices with their start and end apart: 5, of which 1 were waited for; matrix products, arithmetic and copies ran while one was open for 19% of the time, Pallas kernels for 0%

commit v1 on v0

--- a/solution.py
+++ b/solution.py
@@ -2,6 +2,7 @@
 import jax.numpy as jnp
 from jax import lax
 from jax.sharding import PartitionSpec as P
+from jax.lax import all_to_all, axis_size
 
 
 def padded_2(x, sides, width):
@@ -118,13 +119,20 @@
         source_level = moist_field[:, :, source : source + 1, :]
         local_values = local_values + source_level * level_rows[:, source, :]
         inflow = inflow + source_level[:, :, 0, :] * out_row[source]
+    page_divide = lambda target, mesh_name: jnp.concatenate(
+        all_to_all(
+            jnp.stack([target] * axis_size(mesh_name), axis=0),
+            axis_name=mesh_name,
+            split_axis=0,
+            concat_axis=0,
+        ),
+        axis=0,
+    )
     all_flux, all_gain = (
         lax.all_gather(inflow[None].astype(jnp.bfloat16), "gz", axis=0, tiled=True).astype(
             jnp.float32
         ),
-        lax.all_gather(carried_gain[None].astype(jnp.bfloat16), "gz", axis=0, tiled=True).astype(
-            jnp.float32
-        ),
+        page_divide(carried_gain[None].astype(jnp.bfloat16), "gz").astype(jnp.float32),
     )
     height = lax.axis_size("gz")
     own_level = lax.axis_index("gz")

time: 162 us -> 168 us (1.037)
  waiting for transfers between devices: 15.7 us -> 23.8 us
  blocking collectives: 7.95 us -> 0 us
  starting transfers between devices: 8.19 us -> 12.4 us
  local copies, waits for them, and re-layouts: 61.7 us -> 63.5 us
    all_gather x1, waiting for transfers between devices: 15.7 us -> 23.7 us  [body(): lax.all_gather(inflow[None].astype(jnp.bfloat16), 'gz', axis=0, tiled=True)]
    all_gather x1 -> x0, blocking collectives: 7.95 us -> none  [body(): lax.all_gather(carried_gain[None].astype(jnp.bfloat16), 'gz', axis=0, til...]
    all_to_all x0 -> x1, starting transfers between devices: none -> 4.18 us  [body(): all_to_all(jnp.stack([target] * axis_size(mesh_name), axis=0), axis_name=...]
    unnamed x8 -> x7, other arithmetic: 5.05 us -> 3.44 us
  transfers between devices with their start and end apart: 5 -> 6, of which waited for: 1 -> 1; matrix products, arithmetic and copies ran while one was open for 19% -> 60% of each run, Pallas kernels for 0% -> 0%
where the time goes in v1:
time: 168 us
  local copies, waits for them, and re-layouts  63.5 us (38%)
  other arithmetic  50.7 us (30%)
  waiting for transfers between devices  23.8 us (14%)
  between operations  14.3 us (9%)
  starting transfers between devices  12.4 us (7%)
  matrix products  2.91 us (2%)
    slice x1, local copies, waits for them, and re-layouts, body(): source_level = moist_field[:, :, source:source + 1, :]  30.5 us
    all_gather x1, waiting for transfers between devices, body(): lax.all_gather(inflow[None].astype(jnp.bfloat16), 'gz', axis=0, tiled=True)  23.7 us
    scatter-add x1, other arithmetic, body(): moist_field = flat_cells.at[cell_ids].add(tendency.reshape(-1, channels)....  12.7 us
    sub x1, other arithmetic, advect(): centre - jnp.maximum(east_rate, 0.0) * (centre - from_west)  12.5 us
    mul x4, local copies, waits for them, and re-layouts, body(): local_values = local_values + source_level * level_rows[:, source, :]  9.43 us
    convert_element_type x1, other arithmetic, body(): (local_values + incoming[:, :, None, :] * level_gains).astype(jnp.bfloat16)  8.12 us
    unnamed x119, local copies, waits for them, and re-layouts  7.64 us
    gather x1, local copies, waits for them, and re-layouts, body(): flat_cells[cell_ids].astype(jnp.bfloat16)  7.36 us
  transfers between devices with their start and end apart: 6, of which 1 were waited for; matrix products, arithmetic and copies ran while one was open for 60% of the time, Pallas kernels for 0%

profile of v1, /device:TPU:1, one launch (start us, length us, event | category | flops | bytes accessed | tf_op | source)
XLA Modules:
  0.0 167.6 jit_solution(12176542309992120883)
XLA Ops:
  6.5 1.8 %fusion.58 = (bf16[1,32,8,256]{3,2,1,0:T(8,128)(2,1)}, bf16[1,32,8,256]{3,2,1,0:T(8,128)(2,1)}) fusion(bf16[32,32,8,256]{3,2,1,0:T(8,128)(2,1)} %param.10), kind=kLoop, calls=%fused_computation.129 | loop fusion | bytes 524288 | tf_op jit(solution)/shard_map/slice | solution.py:14
  8.3 2.6 %collective-permute-start = (bf16[1,32,8,256]{3,2,1,0:T(8,128)(2,1)}, bf16[1,32,8,256]{3,2,1,0:T(8,128)(2,1)S(1)}, u32[]{:S(2)}, u32[]{:S(2)}) collective-permute-start(bf16[1,32,8,256]{3,2,1,0:T(8,128)(2,1)} %get-tuple-element.24), channel_id=1, source_target_pairs={{0,32},{32,64},{64,96},{96,128},{128,160},{160,192},{192,224},{224... | collective-permute-start | bytes 393224 | tf_op jit(solution)/shard_map/ppermute | solution.py:16
  11.6 1.7 %fusion.57 = (bf16[32,1,8,256]{3,2,1,0:T(8,128)(2,1)}, bf16[32,1,8,256]{3,2,1,0:T(8,128)(2,1)}) fusion(bf16[32,32,8,256]{3,2,1,0:T(8,128)(2,1)} %param.10), kind=kLoop, calls=%fused_computation.128 | loop fusion | bytes 524288 | tf_op jit(solution)/shard_map/slice | solution.py:13
  13.3 1.0 collective-permute-start.2
  14.3 3.9 %collective-permute-start.3 = (bf16[32,1,8,256]{3,2,1,0:T(8,128)(2,1)}, bf16[32,1,8,256]{3,2,1,0:T(8,128)(2,1)}, u32[]{:S(2)}, u32[]{:S(2)}) collective-permute-start(bf16[32,1,8,256]{3,2,1,0:T(8,128)(2,1)} %get-tuple-element.22), channel_id=1, source_target_pairs={{4,0},{8,4},{12,8},{16,12},{20,16},{24,20},{28,24},{0,28},{5,1},{9... | collective-permute-start | bytes 393224 | tf_op jit(solution)/shard_map/ppermute | solution.py:17
  18.2 0.7 add_divide_fusion
  18.9 1.6 convert_reduce_fusion
  22.3 4.2 %all-to-all-start = ((bf16[4,2,128]{2,1,0:T(2,128)(2,1)}), bf16[4,2,128]{2,1,0:T(2,128)(2,1)}, u32[]{:S(2)}, u32[]{:S(2)}) async-start(bf16[4,2,128]{2,1,0:T(2,128)(2,1)} %reshape.2592), calls=%async_computation | async-start | bytes 4096 | tf_op jit(solution)/shard_map/all_to_all | solution.py:123
  27.1 1.6 fusion.61
  30.9 0.9 broadcast_maximum_fusion.1
  32.2 0.9 broadcast_maximum_fusion
  33.6 0.8 copy.43
  34.5 0.7 compare_bitcast_fusion
  35.9 1.6 constant_dynamic-update-slice_fusion.10
  37.5 0.9 multiply_multiply_fusion.1
  39.0 1.4 constant_dynamic-update-slice_fusion.9
  41.0 2.5 %constant_dynamic-update-slice_fusion.1 = bf16[34,32,8,256]{3,2,1,0:T(8,128)(2,1)S(1)} fusion(bf16[34,32,8,256]{3,2,1,0:T(8,128)(2,1)S(1)} %constant_dynamic-update-slice_fusion.2, bf16[32,32,8,256]{3,2,1,0:T(8,128)(2,1)} %param.10), kind=kLoop, calls=%fused_computation.76 | loop fusion | bytes 8388608
  43.6 12.5 %fusion.3 = f32[32,32,8,256]{3,2,1,0:T(8,128)} fusion(bf16[32,32,8,256]{3,2,1,0:T(8,128)(2,1)S(1)} %copy-done.1, bf16[34,32,8,256]{3,2,1,0:T(8,128)(2,1)S(1)} %constant_dynamic-update-slice_fusion, bf16[32,1,8,256]{3,2,1,0:T(8,128)(2,1)} %collective-permute-done.3, bf16[32,1,8,256]{3,2,1,0:T(8,128)(2,1)} %collective-permute-done.2, ...), kind=kLoop, calls=%fused_computation.10 | loop fusion | flops 73400320 | bytes 17694720 | tf_op jit(solution)/shard_map/sub | solution.py:51
  56.1 7.4 %gather_fusion = bf16[1024,256]{1,0:T(8,128)(2,1)S(1)} fusion(f32[8192,256]{1,0:T(8,128)} %bitcast.158, s32[1024]{0:T(1024)} %broadcast_clamp_fusion), kind=kCustom, calls=%fused_computation | custom fusion | bytes 1052672 | tf_op jit(solution)/shard_map/gather | solution.py:97
  63.8 1.3 fusion.64
  65.4 1.0 fusion.26
  66.5 12.7 %scatter_fusion = f32[8192,256]{1,0:T(8,128)} fusion(f32[8192,256]{1,0:T(8,128)} %bitcast.159, s32[1024]{0:T(1024)S(1)} %bitcast.213, f32[1024,256]{1,0:T(8,128)S(1)} %fusion.26), kind=kCustom, calls=%fused_computation.1 | custom fusion | flops 262144 | bytes 3149824 | tf_op jit(solution)/shard_map/scatter-add | solution.py:112
  79.2 30.5 %fusion.56 = (f32[32,32,1,256]{3,2,1,0:T(1,128)S(1)}, f32[32,32,1,256]{3,2,1,0:T(1,128)S(1)}, f32[32,32,1,256]{3,2,1,0:T(1,128)S(1)}, f32[32,32,1,256]{3,2,1,0:T...) fusion(f32[32,32,8,256]{3,2,1,0:T(8,128)} %bitcast.160), kind=kLoop, calls=%fused_computation.127 | loop fusion | bytes 16777216 | tf_op jit(solution)/shard_map/slice | solution.py:119
  110.0 0.7 copy-done.2
  112.5 1.9 %fusion.38 = bf16[1,32,32,256]{3,2,1,0:T(8,128)(2,1)} fusion(f32[32,32,1,256]{3,2,1,0:T(1,128)S(1)} %get-tuple-element.20, f32[32,32,1,256]{3,2,1,0:T(1,128)S(1)} %get-tuple-element.14, f32[32,32,1,256]{3,2,1,0:T(1,128)S(1)} %get-tuple-element.15, f32[32,32,1,256]{3,2,1,0:T(1,128)S(1)} %get-tuple-element.16, f32[32,32,1,256]{3,2,1,0:T(1,128)S(1)} %get-tuple-element.17, ...), kind=kLoop, calls=%fused_computation.45 | loop fusion | flops 4194304 | bytes 8921088 | tf_op jit(solution)/shard_map/convert_element_type | solution.py:132
  116.0 3.3 %copy_bitcast_fusion.6 = (f32[32,32,256]{2,1,0:T(8,128)}, f32[32,32,256]{2,1,0:T(8,128)}) fusion(f32[32,32,1,256]{3,2,1,0:T(1,128)} %copy-done.9, f32[32,32,1,256]{3,2,1,0:T(1,128)} %copy-done.8), kind=kLoop, calls=%fused_computation.66 | loop fusion | bytes 4194304 | tf_op jit(solution)/shard_map/mul | solution.py:120
  119.3 3.1 %copy_bitcast_fusion.4 = (f32[32,32,256]{2,1,0:T(8,128)}, f32[32,32,256]{2,1,0:T(8,128)}) fusion(f32[32,32,1,256]{3,2,1,0:T(1,128)} %copy-done.6, f32[32,32,1,256]{3,2,1,0:T(1,128)} %copy-done.7), kind=kLoop, calls=%fused_computation.64 | loop fusion | bytes 4194304 | tf_op jit(solution)/shard_map/mul | solution.py:120
  122.5 1.5 copy_bitcast_fusion.2
  124.0 1.5 copy_bitcast_fusion
  125.5 23.7 %all-gather.2.cloned.1.call-done = bf16[4,32,32,256]{3,2,1,0:T(8,128)(2,1)} async-done(((bf16[1,32,32,256]{3,2,1,0:T(8,128)(2,1)}), bf16[4,32,32,256]{3,2,1,0:T(8,128)(2,1)}) %all-gather.2.cloned.1.call-update) | async-done | bytes 2097168 | tf_op jit(solution)/shard_map/all_gather | solution.py:132
  149.2 2.2 %convert_element_type.76 = f32[4,32,32,256]{3,2,1,0:T(8,128)S(1)} convert(bf16[4,32,32,256]{3,2,1,0:T(8,128)(2,1)} %all-gather.2.cloned.1.call-done) | non-fusion elementwise | flops 1048576 | bytes 6291456 | tf_op jit(solution)/shard_map/convert_element_type | solution.py:132
  152.6 8.1 %add_convert_fusion = bf16[32,32,8,256]{3,2,1,0:T(8,128)(2,1)} fusion(f32[8,256]{1,0:T(8,128)S(1)} %stack.8, f32[32,32,256]{2,1,0:T(8,128)S(1)} %fusion.36, f32[8,256]{1,0:T(8,128)S(1)} %bitcast.224, f32[32,32,256]{2,1,0:T(8,128)S(1)} %copy-done.16, f32[8,256]{1,0:T(8,128)S(1)} %bitcast.225, f32[32,32,256]{2,1,0:T(8,128)S(1)} %copy-done.17, ...), kind=kLoop, calls=%fused_computation.16 | loop fusion | flops 37748736 | bytes 13705216 | tf_op jit(solution)/shard_map/convert_element_type | solution.py:144
  (157 shorter events, 13.0 us)
Async XLA Ops:
  6.5 57.3 %copy-start = (bf16[256,2048]{1,0:T(8,128)(2,1)S(1)}, bf16[256,2048]{1,0:T(8,128)(2,1)}, u32[]{:S(2)}) copy-start(bf16[256,2048]{1,0:T(8,128)(2,1)} %param.16) | copy-start | bytes 3145732
  8.3 32.7 %collective-permute-start = (bf16[1,32,8,256]{3,2,1,0:T(8,128)(2,1)}, bf16[1,32,8,256]{3,2,1,0:T(8,128)(2,1)S(1)}, u32[]{:S(2)}, u32[]{:S(2)}) collective-permute-start(bf16[1,32,8,256]{3,2,1,0:T(8,128)(2,1)} %get-tuple-element.24), channel_id=1, source_target_pairs={{0,32},{32,64},{64,96},{96,128},{128,160},{160,192},{192,224},{224... | collective-permute-start | bytes 393224 | tf_op jit(solution)/shard_map/ppermute | solution.py:16
  10.9 32.6 %collective-permute-start.1 = (bf16[1,32,8,256]{3,2,1,0:T(8,128)(2,1)}, bf16[1,32,8,256]{3,2,1,0:T(8,128)(2,1)S(1)}, u32[]{:S(2)}, u32[]{:S(2)}) collective-permute-start(bf16[1,32,8,256]{3,2,1,0:T(8,128)(2,1)} %get-tuple-element.23), channel_id=1, source_target_pairs={{32,0},{64,32},{96,64},{128,96},{160,128},{192,160},{224,192},{0,2... | collective-permute-start | bytes 393224 | tf_op jit(solution)/shard_map/ppermute | solution.py:17
  13.3 30.3 %collective-permute-start.2 = (bf16[32,1,8,256]{3,2,1,0:T(8,128)(2,1)}, bf16[32,1,8,256]{3,2,1,0:T(8,128)(2,1)}, u32[]{:S(2)}, u32[]{:S(2)}) collective-permute-start(bf16[32,1,8,256]{3,2,1,0:T(8,128)(2,1)} %get-tuple-element.21), channel_id=1, source_target_pairs={{0,4},{4,8},{8,12},{12,16},{16,20},{20,24},{24,28},{28,0},{1,5},{5... | collective-permute-start | bytes 393224 | tf_op jit(solution)/shard_map/ppermute | solution.py:16
  14.3 29.3 %collective-permute-start.3 = (bf16[32,1,8,256]{3,2,1,0:T(8,128)(2,1)}, bf16[32,1,8,256]{3,2,1,0:T(8,128)(2,1)}, u32[]{:S(2)}, u32[]{:S(2)}) collective-permute-start(bf16[32,1,8,256]{3,2,1,0:T(8,128)(2,1)} %get-tuple-element.22), channel_id=1, source_target_pairs={{4,0},{8,4},{12,8},{16,12},{20,16},{24,20},{28,24},{0,28},{5,1},{9... | collective-permute-start | bytes 393224 | tf_op jit(solution)/shard_map/ppermute | solution.py:17
  22.3 93.0 %all-to-all-start = ((bf16[4,2,128]{2,1,0:T(2,128)(2,1)}), bf16[4,2,128]{2,1,0:T(2,128)(2,1)}, u32[]{:S(2)}, u32[]{:S(2)}) async-start(bf16[4,2,128]{2,1,0:T(2,128)(2,1)} %reshape.2592), calls=%async_computation | async-start | bytes 4096 | tf_op jit(solution)/shard_map/all_to_all | solution.py:123
  26.4 122.7 %all-gather.2.cloned.1.call-start = ((), (), s32[]{:S(2)}) async-start(), calls=%async_computation.1 | async-start | bytes 2621440 | tf_op jit(solution)/shard_map/all_gather | solution.py:132
  34.5 9.0 %copy-start.26 = (s32[1024,1]{0,1:T(1,128)}, s32[1024,1]{0,1:T(1,128)S(1)}, u32[]{:S(2)}) copy-start(s32[1024,1]{0,1:T(1,128)S(1)} %compare_select_fusion) | copy-start | bytes 12292
  35.9 7.7 %copy-start.1 = (bf16[32,32,8,256]{3,2,1,0:T(8,128)(2,1)S(1)}, bf16[32,32,8,256]{3,2,1,0:T(8,128)(2,1)}, u32[]{:S(2)}) copy-start(bf16[32,32,8,256]{3,2,1,0:T(8,128)(2,1)} %param.10) | copy-start | bytes 12582916
  43.6 19.9 %copy-start.19 = (bf16[256,256]{1,0:T(8,128)(2,1)S(1)}, bf16[256,256]{1,0:T(8,128)(2,1)}, u32[]{:S(2)}) copy-start(bf16[256,256]{1,0:T(8,128)(2,1)} %param.18) | copy-start | bytes 393220
  56.1 9.0 %copy-start.20 = (bf16[256,256]{1,0:T(8,128)(2,1)S(1)}, bf16[256,256]{1,0:T(8,128)(2,1)}, u32[]{:S(2)}) copy-start(bf16[256,256]{1,0:T(8,128)(2,1)} %param.19) | copy-start | bytes 393220
  79.2 33.2 %copy-start.37 = (f32[1,256]{1,0:T(1,128)S(1)}, f32[1,256]{1,0:T(1,128)}, u32[]{:S(2)}) copy-start(f32[1,256]{1,0:T(1,128)} %get-tuple-element.37) | copy-start | bytes 3076
  79.2 33.2 %copy-start.38 = (f32[1,256]{1,0:T(1,128)S(1)}, f32[1,256]{1,0:T(1,128)}, u32[]{:S(2)}) copy-start(f32[1,256]{1,0:T(1,128)} %get-tuple-element.38) | copy-start | bytes 3076
  79.2 33.2 %copy-start.39 = (f32[1,256]{1,0:T(1,128)S(1)}, f32[1,256]{1,0:T(1,128)}, u32[]{:S(2)}) copy-start(f32[1,256]{1,0:T(1,128)} %get-tuple-element.39) | copy-start | bytes 3076
  79.2 33.2 %copy-start.40 = (f32[1,256]{1,0:T(1,128)S(1)}, f32[1,256]{1,0:T(1,128)}, u32[]{:S(2)}) copy-start(f32[1,256]{1,0:T(1,128)} %get-tuple-element.40) | copy-start | bytes 3076
  79.2 33.2 %copy-start.41 = (f32[1,256]{1,0:T(1,128)S(1)}, f32[1,256]{1,0:T(1,128)}, u32[]{:S(2)}) copy-start(f32[1,256]{1,0:T(1,128)} %get-tuple-element.41) | copy-start | bytes 3076
  79.2 33.2 %copy-start.42 = (f32[1,256]{1,0:T(1,128)S(1)}, f32[1,256]{1,0:T(1,128)}, u32[]{:S(2)}) copy-start(f32[1,256]{1,0:T(1,128)} %get-tuple-element.42) | copy-start | bytes 3076
  79.2 33.2 %copy-start.43 = (f32[1,256]{1,0:T(1,128)S(1)}, f32[1,256]{1,0:T(1,128)}, u32[]{:S(2)}) copy-start(f32[1,256]{1,0:T(1,128)} %get-tuple-element.43) | copy-start | bytes 3076
  79.2 33.2 %copy-start.44 = (f32[1,256]{1,0:T(1,128)S(1)}, f32[1,256]{1,0:T(1,128)}, u32[]{:S(2)}) copy-start(f32[1,256]{1,0:T(1,128)} %get-tuple-element.44) | copy-start | bytes 3076
  109.8 4.6 %copy-start.21 = (f32[8,8,256]{2,1,0:T(8,128)S(1)}, f32[8,8,256]{2,1,0:T(8,128)}, u32[]{:S(2)}) copy-start(f32[8,8,256]{2,1,0:T(8,128)} %constant_dynamic-update-slice_fusion.9) | copy-start | bytes 196612
  109.8 4.6 %copy-start.22 = (f32[1,256]{1,0:T(1,128)S(1)}, f32[1,256]{1,0:T(1,128)}, u32[]{:S(2)}) copy-start(f32[1,256]{1,0:T(1,128)} %get-tuple-element.46) | copy-start | bytes 3076
  109.9 5.3 %copy-start.46 = (f32[1,256]{1,0:T(1,128)S(1)}, f32[1,256]{1,0:T(1,128)}, u32[]{:S(2)}) copy-start(f32[1,256]{1,0:T(1,128)} %get-tuple-element.6) | copy-start | bytes 3076
  109.9 5.3 %copy-start.47 = (f32[1,256]{1,0:T(1,128)S(1)}, f32[1,256]{1,0:T(1,128)}, u32[]{:S(2)}) copy-start(f32[1,256]{1,0:T(1,128)} %get-tuple-element.7) | copy-start | bytes 3076
  109.9 5.3 %copy-start.48 = (f32[1,256]{1,0:T(1,128)S(1)}, f32[1,256]{1,0:T(1,128)}, u32[]{:S(2)}) copy-start(f32[1,256]{1,0:T(1,128)} %get-tuple-element.8) | copy-start | bytes 3076
  109.9 5.3 %copy-start.49 = (f32[1,256]{1,0:T(1,128)S(1)}, f32[1,256]{1,0:T(1,128)}, u32[]{:S(2)}) copy-start(f32[1,256]{1,0:T(1,128)} %get-tuple-element.9) | copy-start | bytes 3076
  110.0 5.3 %copy-start.50 = (f32[1,256]{1,0:T(1,128)S(1)}, f32[1,256]{1,0:T(1,128)}, u32[]{:S(2)}) copy-start(f32[1,256]{1,0:T(1,128)} %get-tuple-element.10) | copy-start | bytes 3076
  110.0 5.3 %copy-start.51 = (f32[1,256]{1,0:T(1,128)S(1)}, f32[1,256]{1,0:T(1,128)}, u32[]{:S(2)}) copy-start(f32[1,256]{1,0:T(1,128)} %get-tuple-element.11) | copy-start | bytes 3076
  110.0 5.3 %copy-start.52 = (f32[1,256]{1,0:T(1,128)S(1)}, f32[1,256]{1,0:T(1,128)}, u32[]{:S(2)}) copy-start(f32[1,256]{1,0:T(1,128)} %get-tuple-element.12) | copy-start | bytes 3076
  116.0 6.5 %copy-start.3 = (f32[32,32,1,256]{3,2,1,0:T(1,128)S(1)}, f32[32,32,1,256]{3,2,1,0:T(1,128)}, u32[]{:S(2)}) copy-start(f32[32,32,1,256]{3,2,1,0:T(1,128)} %copy-done.2) | copy-start | bytes 3145732
  116.0 6.5 %copy-start.5 = (f32[32,32,1,256]{3,2,1,0:T(1,128)S(1)}, f32[32,32,1,256]{3,2,1,0:T(1,128)}, u32[]{:S(2)}) copy-start(f32[32,32,1,256]{3,2,1,0:T(1,128)} %copy-done.4) | copy-start | bytes 3145732
  125.5 26.6 %copy-start.10 = (f32[32,32,256]{2,1,0:T(8,128)S(1)}, f32[32,32,256]{2,1,0:T(8,128)}, u32[]{:S(2)}) copy-start(f32[32,32,256]{2,1,0:T(8,128)} %get-tuple-element.78) | copy-start | bytes 3145732
  125.5 26.6 %copy-start.11 = (f32[32,32,256]{2,1,0:T(8,128)S(1)}, f32[32,32,256]{2,1,0:T(8,128)}, u32[]{:S(2)}) copy-start(f32[32,32,256]{2,1,0:T(8,128)} %get-tuple-element.79) | copy-start | bytes 3145732
  (27 other events, 90.0 us)
Sparse Core Ops, SparseCore 0:
  114.5 34.6 all-gather.1
